TPU v7x, 512 devices: a whole 4x8x8 slice. The times are simulated.
512 devices in a mesh: grp: 32 (over y, z_hi, core), leaf: 16 (over z_lo, x).
Axes of the slice: x: 4, y: 8, z: 8 (z_hi: 2, z_lo: 4; z = z_hi * 4 + z_lo), core: 2. Of those that a mesh axis runs over, the one named last changes fastest.
Arguments:
- vectors: bfloat16 [32, 2097152], P(None, ('grp', 'leaf')), may hold values from -6 to 6
- offsets: bfloat16 [3, 2097152], P(None, ('grp', 'leaf')), may hold values from 0 to 1
- near_list: int32 [8192, 16], P(('grp', 'leaf')), may hold values from 0 to 8191, as said below
- near_count: int32 [8192], P(('grp', 'leaf')), may hold values from 8 to 16, as said below
- leaf_basis: bfloat16 [8192, 64, 256], P(('grp', 'leaf')), may hold values from -0.375 to 0.375
- far_list: int32 [8192, 16], P(('grp', 'leaf')), may hold values from 0 to 8191, as said below
- far_count: int32 [8192], P(('grp', 'leaf')), may hold values from 0 to 16, as said below
- leaf_coupling: bfloat16 [8192, 16, 64, 64], P(('grp', 'leaf')), as said below
- transfer: bfloat16 [8192, 64, 64], P(('grp', 'leaf')), may hold values from -0.75 to 0.75
- group_list: int32 [32, 16], P('grp'), may hold values from 0 to 31, as said below
- group_count: int32 [32], P('grp'), may hold values from 8 to 16, as said below
- group_coupling: bfloat16 [32, 16, 64, 64], P('grp', 'leaf'), may hold values from -0.01171875 to 0.01171875
Outputs:
- applied: bfloat16 [32, 2097152], P(None, ('grp', 'leaf'))
Inputs may be any that keep to these rules, and one draw needn't show every extreme that they name: `near_list`: the first near_count[l] entries of row l are distinct leaves of l's own group lying on l's device or on the devices just before and after it along leaf (16 consecutive leaves a device); the first entry is l itself and the remaining entries repeat l. `near_count`: the first leaf of every device has exactly 16. `far_list`: the first far_count[l] entries of row l are distinct leaves of l's own group other than l; the remaining entries repeat l. If leaf j stands in slot k < far_count[l] of row l, then l stands in some slot k2 < far_count[j] of row j. `far_count`: the first leaf of every group has exactly 16. If far_list[l, k] = j with k < far_count[l], and far_list[j, k2] = l with k2 < far_count[j], then leaf_coupling[j, k2] is the transpose of leaf_coupling[l, k]. `group_list`: the first group_count[g] entries of row g are distinct groups other than g; the remaining entries repeat g. `group_count`: group 0 has exactly 16.
All inputs are finite; a program needn't handle non-finite values.
Results may differ from a plain program's by a relative error of at most 0.005.
Values may be sent and summed in bfloat16 or wider, within the bound.
No kernel may reach another device: no remote copies, remote signals or barrier semaphores. Data moves between devices by JAX's collectives and lax.ppermute only.
A program may use at most 64 MiB of HBM per device.

v0:
```python
import jax
import jax.numpy as jnp
from jax import lax
from jax.sharding import PartitionSpec as P

inv_four_pi = 0.07957747154594767
soften = 0.01


def with_halo(shard, sides, width):
    for axis, dim in sides:
        count, length = (lax.axis_size(axis), shard.shape[dim])
        up = [(i, (i + 1) % count) for i in range(count - 1)]
        down = [(j, i) for i, j in up]
        last = lax.slice_in_dim(shard, length - width, length, axis=dim)
        first = lax.slice_in_dim(shard, 0, width, axis=dim)
        before = lax.ppermute(last, axis, up)
        after = lax.ppermute(first, axis, down)
        shard = jnp.concatenate([before, shard, after], axis=dim)
    return shard


def centres(leaf_ids):
    columns = []
    for axis_pos in range(3):
        summed = jnp.zeros_like(leaf_ids)
        for bit_pos in range(10):
            picked = jnp.bitwise_and(jnp.right_shift(leaf_ids, 3 * bit_pos + axis_pos), 1)
            summed = summed + jnp.left_shift(picked, bit_pos)
        columns.append(summed.astype(jnp.float32))
    return jnp.stack(columns)


def kernel_tile(source_pts, target_pts):
    squared = jnp.zeros(
        (source_pts.shape[0], source_pts.shape[2], target_pts.shape[1]), jnp.float32
    )
    for axis_pos in range(3):
        spacing = source_pts[:, axis_pos, :, None] - target_pts[axis_pos][None, None, :]
        squared = squared + spacing * spacing
    return inv_four_pi * lax.rsqrt(squared + soften)


def body(
    vectors,
    offsets,
    near_list,
    near_count,
    leaf_basis,
    far_list,
    far_count,
    leaf_coupling,
    transfer,
    group_list,
    group_count,
    group_coupling,
):
    leaf_devices = lax.axis_size("leaf")
    local_leaves = near_list.shape[0]
    near_slots = near_list.shape[1]
    far_slots = far_list.shape[1]
    vec_count = vectors.shape[0]
    leaf_width = vectors.shape[1] // local_leaves
    group_leaves = leaf_devices * local_leaves
    leaf_place = lax.axis_index("leaf")
    group_place = lax.axis_index("grp")
    device_first = (group_place * leaf_devices + leaf_place) * local_leaves
    group_first = group_place * group_leaves
    window_first = device_first - local_leaves
    stacked = jnp.concatenate([vectors, offsets], axis=0)
    widened = with_halo(stacked, (("leaf", 1),), local_leaves * leaf_width)
    window_vectors = widened[:vec_count].reshape(vec_count, 3 * local_leaves, leaf_width)
    window_ids = window_first + jnp.arange(3 * local_leaves, dtype=jnp.int32)
    window_pts = (
        widened[vec_count:].astype(jnp.float32).reshape(3, 3 * local_leaves, leaf_width)
        + centres(window_ids)[:, :, None]
    )
    slot_ids = jnp.arange(near_slots, dtype=jnp.int32)

    def near_step(running, target):
        sources = near_list[target] - window_first
        active_slots = slot_ids < near_count[target]
        source_pts = jnp.take(window_pts, sources, axis=1).transpose(1, 0, 2)
        target_pts = lax.dynamic_index_in_dim(window_pts, local_leaves + target, 1, keepdims=False)
        near_tile = jnp.where(
            active_slots[:, None, None], kernel_tile(source_pts, target_pts), 0.0
        ).astype(jnp.bfloat16)
        source_vectors = jnp.take(window_vectors, sources, axis=1)
        return (
            running,
            jnp.einsum(
                "vkb,kba->va", source_vectors, near_tile, preferred_element_type=jnp.float32
            ),
        )

    ignored, near_field = lax.scan(near_step, 0, jnp.arange(local_leaves, dtype=jnp.int32))
    leaf_vectors = vectors.reshape(vec_count, local_leaves, leaf_width)
    coeffs = jnp.einsum(
        "via,ira->ivr", leaf_vectors, leaf_basis, preferred_element_type=jnp.float32
    ).astype(jnp.bfloat16)
    far_active = jnp.arange(far_slots, dtype=jnp.int32)[None, :] < far_count[:, None]
    far_rows = far_list - group_first
    group_coeffs = lax.all_gather(coeffs, "leaf", axis=0, tiled=True)
    picked = jnp.take(group_coeffs, far_rows, axis=0)
    picked = jnp.where(far_active[:, :, None, None], picked, jnp.zeros((), jnp.bfloat16))
    far_field = jnp.einsum(
        "ikvs,ikrs->ivr", picked, leaf_coupling, preferred_element_type=jnp.float32
    )
    coarse_part = jnp.einsum("ivs,isr->vr", coeffs, transfer, preferred_element_type=jnp.float32)
    coarse = lax.psum(coarse_part, "leaf").astype(jnp.bfloat16)
    all_coarse = lax.all_gather(coarse[None], "grp", axis=0, tiled=True)
    group_active = jnp.arange(group_list.shape[1], dtype=jnp.int32) < group_count[0]
    own_slots = group_coupling.shape[1]
    slot_first = leaf_place * own_slots
    own_groups = lax.dynamic_slice_in_dim(group_list[0], slot_first, own_slots, 0)
    own_active = lax.dynamic_slice_in_dim(group_active, slot_first, own_slots, 0)
    picked_groups = jnp.where(
        own_active[:, None, None],
        jnp.take(all_coarse, own_groups, axis=0),
        jnp.zeros((), jnp.bfloat16),
    )
    coarse_term = jnp.einsum(
        "kvs,krs->vr", picked_groups, group_coupling[0], preferred_element_type=jnp.float32
    )
    coarse_out = lax.psum(coarse_term, "leaf")
    downward = jnp.einsum(
        "vs,irs->ivr", coarse_out.astype(jnp.bfloat16), transfer, preferred_element_type=jnp.float32
    )
    local_coeffs = (far_field + downward).astype(jnp.bfloat16)
    expanded = jnp.einsum(
        "ivr,ira->via", local_coeffs, leaf_basis, preferred_element_type=jnp.float32
    )
    result = jnp.transpose(near_field, (1, 0, 2)) + expanded
    return result.reshape(vec_count, local_leaves * leaf_width).astype(jnp.bfloat16)


def solution(mesh):
    placed = (
        P(None, ("grp", "leaf")),
        P(None, ("grp", "leaf")),
        P(("grp", "leaf"), None),
        P(("grp", "leaf")),
        P(("grp", "leaf"), None, None),
        P(("grp", "leaf"), None),
        P(("grp", "leaf")),
        P(("grp", "leaf"), None, None, None),
        P(("grp", "leaf"), None, None),
        P("grp", None),
        P("grp"),
        P("grp", "leaf", None, None),
    )
    return jax.shard_map(
        body, mesh=mesh, in_specs=placed, out_specs=P(None, ("grp", "leaf")), check_vma=False
    )
```

profile of v0, /device:TPU:8, one launch (start us, length us, event | category | flops | bytes accessed | tf_op | source)
XLA Modules:
  0.0 398.0 jit_solution(17522042291182980777)
XLA Ops:
  6.5 1.0 constant_dynamic-update-slice_fusion.1
  7.6 0.8 constant_dynamic-update-slice_fusion
  8.4 1.3 collective-permute-start.1
  9.7 4.6 %collective-permute-start = (bf16[35,4096]{1,0:T(8,128)(2,1)S(1)}, bf16[35,4096]{1,0:T(8,128)(2,1)S(1)}, u32[]{:S(2)}, u32[]{:S(2)}) collective-permute-start(bf16[35,4096]{1,0:T(8,128)(2,1)S(1)} %constant_dynamic-update-slice_fusion), channel_id=1, source_target_pairs={{0,1},{1,2},{2,3},{3,4},{4,5},{5,6},{6,7},{7,8},{8,9},{9,10},{10,1... | collective-permute-start | bytes 860168 | tf_op jit(solution)/shard_map/ppermute | solution.py:17
  14.3 1.9 convolution_convert_fusion
  17.5 1.2 constant_dynamic-slice_fusion.4
  20.4 0.7 compare_and_fusion.1
  21.3 1.2 convolution_bitcast_fusion.1
  22.5 80.5 %psum.14 = bf16[32,64]{1,0:T(8,128)(2,1)S(1)} all-reduce(f32[32,64]{1,0:T(8,128)S(1)} %convolution_bitcast_fusion.1), channel_id=1, replica_groups=mesh['grp'=32,'leaf'=16] {'leaf'}, use_global_device_ids=true, to_apply=%region_2.3 | all-reduce | flops 2048 | bytes 12288 | tf_op jit(solution)/shard_map/psum | solution.py:110
  103.0 53.7 %all-gather = bf16[1024,64]{1,0:T(8,128)(2,1)S(1)} all-gather(bf16[32,64]{1,0:T(8,128)(2,1)S(1)} %psum.14), channel_id=2, replica_groups=mesh['grp'=32,'leaf'=16] {'grp'}, dimensions={0}, use_global_device_ids=true | all-gather | bytes 135168 | tf_op jit(solution)/shard_map/all_gather | solution.py:111
  156.7 1.5 fusion.30
  158.2 74.2 %psum.15 = bf16[32,64]{1,0:T(8,128)(2,1)S(1)} all-reduce(f32[32,64]{1,0:T(8,128)S(1)} %fusion.30), channel_id=1, replica_groups=mesh['grp'=32,'leaf'=16] {'leaf'}, use_global_device_ids=true, to_apply=%region_3.4 | all-reduce | flops 2048 | bytes 12288 | tf_op jit(solution)/shard_map/psum | solution.py:125
  232.5 0.7 iota_compare_fusion
  233.6 148.9 %while.15 = (s32[]{:T(128)}, f32[16,32,256]{2,1,0:T(8,128)S(1)}, s32[16]{0:T(128)S(1)}, s32[16,16]{1,0:T(8,128)}, s32[]{:T(128)}, /*index=5*/bf16[32,48,256]{2,0...) while((s32[]{:T(128)}, f32[16,32,256]{2,1,0:T(8,128)S(1)}, ...), condition=%wide.region_1.2_spmd.clone, body=%wide.region_0.1_spmd.clone.sunk | while | flops 79836360 | bytes 1276693 | solution.py:96
  237.7 0.7 fusion.60
  238.3 1.4 compare_and_fusion.3
  241.1 1.9 fusion.62
  247.0 0.7 fusion.60
  247.7 1.4 compare_and_fusion.3
  250.4 1.9 fusion.62
  256.3 0.7 fusion.60
  257.0 1.4 compare_and_fusion.3
  259.7 1.9 fusion.62
  265.6 0.7 fusion.60
  266.3 1.4 compare_and_fusion.3
  269.0 1.9 fusion.62
  274.9 0.7 fusion.60
  275.6 1.4 compare_and_fusion.3
  278.3 1.9 fusion.62
  284.2 0.7 fusion.60
  284.9 1.4 compare_and_fusion.3
  287.6 1.9 fusion.62
  293.5 0.7 fusion.60
  294.2 1.4 compare_and_fusion.3
  296.9 1.9 fusion.62
  302.8 0.7 fusion.60
  303.5 1.4 compare_and_fusion.3
  306.2 1.9 fusion.62
  312.1 0.7 fusion.60
  312.8 1.4 compare_and_fusion.3
  315.6 1.9 fusion.62
  321.4 0.7 fusion.60
  322.1 1.4 compare_and_fusion.3
  324.9 1.9 fusion.62
  330.7 0.7 fusion.60
  331.4 1.4 compare_and_fusion.3
  334.2 1.9 fusion.62
  340.0 0.7 fusion.60
  340.7 1.4 compare_and_fusion.3
  343.5 1.9 fusion.62
  350.0 1.4 compare_and_fusion.3
  352.8 1.9 fusion.62
  359.3 1.4 compare_and_fusion.3
  362.1 1.9 fusion.62
  368.0 0.7 fusion.60
  368.7 1.4 compare_and_fusion.3
  371.4 1.9 fusion.62
  377.3 0.7 fusion.60
  378.0 1.4 compare_and_fusion.3
  380.7 1.9 fusion.62
  382.6 2.6 gather_fusion.2
  385.2 3.8 fusion.20
  389.0 1.4 fusion.23
  390.4 0.7 copy.30
  (204 shorter events, 44.5 us)
Async XLA Ops:
  6.5 7.7 %copy-start = (bf16[16,64,256]{2,1,0:T(8,128)(2,1)S(1)}, bf16[16,64,256]{2,1,0:T(8,128)(2,1)}, u32[]{:S(2)}) copy-start(bf16[16,64,256]{2,1,0:T(8,128)(2,1)} %param.18) | copy-start | bytes 1572868
  6.5 376.0 %all-gather.3.cloned.1.call-start = ((), (), s32[]{:S(2)}) async-start(), calls=%async_computation | async-start | bytes 2228224 | tf_op jit(solution)/shard_map/all_gather | solution.py:103
  8.4 224.9 %collective-permute-start.1 = (bf16[35,4096]{1,0:T(8,128)(2,1)S(1)}, bf16[35,4096]{1,0:T(8,128)(2,1)S(1)}, u32[]{:S(2)}, u32[]{:S(2)}) collective-permute-start(bf16[35,4096]{1,0:T(8,128)(2,1)S(1)} %constant_dynamic-update-slice_fusion), channel_id=1, source_target_pairs={{1,0},{2,1},{3,2},{4,3},{5,4},{6,5},{7,6},{8,7},{9,8},{10,9},{11,1... | collective-permute-start | bytes 860168 | tf_op jit(solution)/shard_map/ppermute | solution.py:18
  9.7 223.6 %collective-permute-start = (bf16[35,4096]{1,0:T(8,128)(2,1)S(1)}, bf16[35,4096]{1,0:T(8,128)(2,1)S(1)}, u32[]{:S(2)}, u32[]{:S(2)}) collective-permute-start(bf16[35,4096]{1,0:T(8,128)(2,1)S(1)} %constant_dynamic-update-slice_fusion), channel_id=1, source_target_pairs={{0,1},{1,2},{2,3},{3,4},{4,5},{5,6},{6,7},{7,8},{8,9},{9,10},{10,1... | collective-permute-start | bytes 860168 | tf_op jit(solution)/shard_map/ppermute | solution.py:17
  14.2 219.4 %copy-start.2 = (s32[16]{0:T(128)S(1)}, s32[16]{0:T(128)}, u32[]{:S(2)}) copy-start(s32[16]{0:T(128)} %param.17) | copy-start | bytes 196
  385.2 3.8 copy-start.1
Sparse Core Ops, SparseCore 0:
  16.3 92.5 all-gather.2
where the time goes:
time: 400 us; the launch traced here: 398 us
  blocking collectives  208 us (52%)
  local copies, waits for them, and re-layouts  47.7 us (12%)
  loops' own time  44.3 us (11%)
  matrix products  39.6 us (10%)
  other arithmetic  36.2 us (9%)
  between operations  15.9 us (4%)
  starting transfers between devices  5.86 us (1%)
    psum x1, blocking collectives, body(): coarse = lax.psum(coarse_part, 'leaf').astype(jnp.bfloat16)  80.5 us
    psum x1, blocking collectives, body(): coarse_out = lax.psum(coarse_term, 'leaf')  74.2 us
    all_gather x1, blocking collectives, body(): all_coarse = lax.all_gather(coarse[None], 'grp', axis=0, tiled=True)  53.7 us
    another operation x1, loops' own time, body(): lax.scan(near_step, 0, jnp.arange(local_leaves, dtype=jnp.int32))  44.3 us
    dot_general x16, matrix products, near_step(): jnp.einsum('vkb,kba->va', source_vectors, near_tile, preferred_element_ty...  29.8 us
    and x16, other arithmetic, near_step(): source_vectors = jnp.take(window_vectors, sources, axis=1)  21.9 us
    select_n x16, other arithmetic, near_step(): source_vectors = jnp.take(window_vectors, sources, axis=1)  11.1 us
    dynamic_slice x16, local copies, waits for them, and re-layouts, body(): lax.scan(near_step, 0, jnp.arange(local_leaves, dtype=jnp.int32))  10.5 us
  transfers between devices with their start and end apart: 3, of which 0 were waited for; matrix products, arithmetic and copies ran while one was open for 28% of the time, Pallas kernels for 0%

commit v1 on v0

--- a/solution.py
+++ b/solution.py
@@ -108,7 +108,9 @@
     )
     coarse_part = jnp.einsum("ivs,isr->vr", coeffs, transfer, preferred_element_type=jnp.float32)
     coarse = lax.psum(coarse_part, "leaf").astype(jnp.bfloat16)
-    all_coarse = lax.all_gather(coarse[None], "grp", axis=0, tiled=True)
+    all_coarse = jnp.concatenate(
+        lax.all_to_all(jnp.stack([coarse[None]] * lax.axis_size("grp")), "grp", 0, 0), axis=0
+    )
     group_active = jnp.arange(group_list.shape[1], dtype=jnp.int32) < group_count[0]
     own_slots = group_coupling.shape[1]
     slot_first = leaf_place * own_slots

time: 400 us -> 368 us (0.920)
  blocking collectives: 208 us -> 155 us
  starting transfers between devices: 5.86 us -> 19.3 us
  waiting for transfers between devices: 0.03 us -> 6.85 us
    all_gather x1 -> x0, blocking collectives: 53.7 us -> none  [body(): all_coarse = lax.all_gather(coarse[None], 'grp', axis=0, tiled=True)]
    all_to_all x0 -> x1, starting transfers between devices: none -> 13.5 us  [body(): lax.all_to_all(jnp.stack([coarse[None]] * lax.axis_size('grp')), 'grp', 0...]
    all_to_all x0 -> x1, waiting for transfers between devices: none -> 6.83 us  [body(): lax.all_to_all(jnp.stack([coarse[None]] * lax.axis_size('grp')), 'grp', 0...]
  transfers between devices with their start and end apart: 3 -> 4, of which waited for: 0 -> 1; matrix products, arithmetic and copies ran while one was open for 28% -> 31% of each run, Pallas kernels for 0% -> 0%
where the time goes in v1:
time: 368 us; the launch traced here: 366 us
  blocking collectives  155 us (42%)
  local copies, waits for them, and re-layouts  48.7 us (13%)
  loops' own time  44.3 us (12%)
  matrix products  39.6 us (11%)
  other arithmetic  36.2 us (10%)
  starting transfers between devices  19.3 us (5%)
  between operations  16.1 us (4%)
  waiting for transfers between devices  6.85 us (2%)
    psum x1, blocking collectives, body(): coarse = lax.psum(coarse_part, 'leaf').astype(jnp.bfloat16)  80.5 us
    psum x1, blocking collectives, body(): coarse_out = lax.psum(coarse_term, 'leaf')  74.3 us
    another operation x1, loops' own time, body(): lax.scan(near_step, 0, jnp.arange(local_leaves, dtype=jnp.int32))  44.3 us
    dot_general x16, matrix products, near_step(): jnp.einsum('vkb,kba->va', source_vectors, near_tile, preferred_element_ty...  29.8 us
    and x16, other arithmetic, near_step(): source_vectors = jnp.take(window_vectors, sources, axis=1)  21.9 us
    all_to_all x1, starting transfers between devices, body(): lax.all_to_all(jnp.stack([coarse[None]] * lax.axis_size('grp')), 'grp', 0...  13.5 us
    select_n x16, other arithmetic, near_step(): source_vectors = jnp.take(window_vectors, sources, axis=1)  11.1 us
    dynamic_slice x16, local copies, waits for them, and re-layouts, body(): lax.scan(near_step, 0, jnp.arange(local_leaves, dtype=jnp.int32))  10.5 us
  transfers between devices with their start and end apart: 4, of which 1 were waited for; matrix products, arithmetic and copies ran while one was open for 31% of the time, Pallas kernels for 0%

profile of v1, /device:TPU:8, one launch (start us, length us, event | category | flops | bytes accessed | tf_op | source)
XLA Modules:
  0.0 365.8 jit_solution(73190281715758642)
XLA Ops:
  6.5 1.0 constant_dynamic-update-slice_fusion.1
  7.6 0.8 constant_dynamic-update-slice_fusion
  8.4 1.3 collective-permute-start.1
  9.7 4.6 %collective-permute-start = (bf16[35,4096]{1,0:T(8,128)(2,1)S(1)}, bf16[35,4096]{1,0:T(8,128)(2,1)S(1)}, u32[]{:S(2)}, u32[]{:S(2)}) collective-permute-start(bf16[35,4096]{1,0:T(8,128)(2,1)S(1)} %constant_dynamic-update-slice_fusion), channel_id=1, source_target_pairs={{0,1},{1,2},{2,3},{3,4},{4,5},{5,6},{6,7},{7,8},{8,9},{9,10},{10,1... | collective-permute-start | bytes 860168 | tf_op jit(solution)/shard_map/ppermute | solution.py:17
  14.2 1.9 convolution_convert_fusion
  16.2 1.2 convolution_bitcast_fusion.1
  17.4 80.5 %psum.14 = bf16[32,64]{1,0:T(8,128)(2,1)S(1)} all-reduce(f32[32,64]{1,0:T(8,128)S(1)} %convolution_bitcast_fusion.1), channel_id=1, replica_groups=mesh['grp'=32,'leaf'=16] {'leaf'}, use_global_device_ids=true, to_apply=%region_2.3 | all-reduce | flops 2048 | bytes 12288 | tf_op jit(solution)/shard_map/psum | solution.py:110
  98.0 0.8 reshape.569
  98.8 13.5 %all-to-all-start = ((bf16[32,2,1024]{2,1,0:T(2,128)(2,1)}), bf16[32,2,1024]{2,1,0:T(2,128)(2,1)S(1)}, u32[]{:S(2)}, u32[]{:S(2)}) async-start(bf16[32,2,1024]{2,1,0:T(2,128)(2,1)} %reshape.569), calls=%async_computation | async-start | bytes 262144 | tf_op jit(solution)/shard_map/all_to_all | solution.py:112
  112.4 0.7 iota_compare_fusion
  113.1 0.7 compare_and_fusion.1
  115.2 1.2 constant_dynamic-slice_fusion.4
  118.4 6.8 %all-to-all-done = bf16[32,2,1024]{2,1,0:T(2,128)(2,1)S(1)} async-done(((bf16[32,2,1024]{2,1,0:T(2,128)(2,1)}), bf16[32,2,1024]{2,1,0:T(2,128)(2,1)S(1)}, u32[]{:S(2)}, u32[]{:S(2)}) %all-to-all-start) | async-done | bytes 131104 | tf_op jit(solution)/shard_map/all_to_all | solution.py:112
  125.4 1.4 fusion.30
  126.8 74.3 %psum.15 = bf16[32,64]{1,0:T(8,128)(2,1)S(1)} all-reduce(f32[32,64]{1,0:T(8,128)S(1)} %fusion.30), channel_id=1, replica_groups=mesh['grp'=32,'leaf'=16] {'leaf'}, use_global_device_ids=true, to_apply=%region_3.4 | all-reduce | flops 2048 | bytes 12288 | tf_op jit(solution)/shard_map/psum | solution.py:127
  201.5 148.8 %while.15 = (s32[]{:T(128)}, f32[16,32,256]{2,1,0:T(8,128)S(1)}, s32[16]{0:T(128)S(1)}, s32[16,16]{1,0:T(8,128)}, s32[]{:T(128)}, /*index=5*/bf16[32,48,256]{2,0...) while((s32[]{:T(128)}, f32[16,32,256]{2,1,0:T(8,128)S(1)}, ...), condition=%wide.region_1.2_spmd.clone, body=%wide.region_0.1_spmd.clone.sunk | while | flops 79836360 | bytes 1276693 | solution.py:96
  205.6 0.7 fusion.61
  206.2 1.4 compare_and_fusion.3
  209.0 1.9 fusion.63
  214.9 0.7 fusion.61
  215.5 1.4 compare_and_fusion.3
  218.3 1.9 fusion.63
  224.2 0.7 fusion.61
  224.8 1.4 compare_and_fusion.3
  227.6 1.9 fusion.63
  233.5 0.7 fusion.61
  234.2 1.4 compare_and_fusion.3
  236.9 1.9 fusion.63
  242.8 0.7 fusion.61
  243.5 1.4 compare_and_fusion.3
  246.2 1.9 fusion.63
  252.1 0.7 fusion.61
  252.8 1.4 compare_and_fusion.3
  255.5 1.9 fusion.63
  261.4 0.7 fusion.61
  262.1 1.4 compare_and_fusion.3
  264.8 1.9 fusion.63
  270.7 0.7 fusion.61
  271.4 1.4 compare_and_fusion.3
  274.1 1.9 fusion.63
  280.7 1.4 compare_and_fusion.3
  283.4 1.9 fusion.63
  290.0 1.4 compare_and_fusion.3
  292.7 1.9 fusion.63
  298.6 0.7 fusion.61
  299.3 1.4 compare_and_fusion.3
  302.0 1.9 fusion.63
  307.9 0.7 fusion.61
  308.6 1.4 compare_and_fusion.3
  311.3 1.9 fusion.63
  317.2 0.7 fusion.61
  317.9 1.4 compare_and_fusion.3
  320.6 1.9 fusion.63
  327.2 1.4 compare_and_fusion.3
  329.9 1.9 fusion.63
  336.5 1.4 compare_and_fusion.3
  339.2 1.9 fusion.63
  345.1 0.7 fusion.61
  345.8 1.4 compare_and_fusion.3
  348.5 1.9 fusion.63
  350.4 2.6 gather_fusion.2
  353.0 3.8 %fusion.20 = f32[16,32,64]{2,1,0:T(8,128)} fusion(bf16[16,16,64,64]{3,2,1,0:T(8,128)(2,1)} %param.21, bf16[16,16,32,64]{3,2,1,0:T(8,128)(2,1)S(1)} %bitcast.106, pred[16,16]{1,0:T(8,128)(4,1)S(1)} %get-tuple-element.195, pred[16,16]{1,0:T(8,128)(4,1)S(1)} %iota_compare_fusion), kind=kOutput, calls=%fused_computation.38 | convolution fusion | flops 68157440 | bytes 3277312 | tf_op jit(solution)/shard_map/ikvs,ikrs->ivr/dot_general | solution.py:106
  356.8 1.4 fusion.23
  358.3 0.7 copy.30
  (208 shorter events, 46.0 us)
Async XLA Ops:
  6.5 7.7 %copy-start = (bf16[16,64,256]{2,1,0:T(8,128)(2,1)S(1)}, bf16[16,64,256]{2,1,0:T(8,128)(2,1)}, u32[]{:S(2)}) copy-start(bf16[16,64,256]{2,1,0:T(8,128)(2,1)} %param.18) | copy-start | bytes 1572868
  6.5 343.8 %all-gather.2.cloned.1.call-start = ((), (), s32[]{:S(2)}) async-start(), calls=%async_computation.1 | async-start | bytes 2228224 | tf_op jit(solution)/shard_map/all_gather | solution.py:103
  8.4 192.8 %collective-permute-start.1 = (bf16[35,4096]{1,0:T(8,128)(2,1)S(1)}, bf16[35,4096]{1,0:T(8,128)(2,1)S(1)}, u32[]{:S(2)}, u32[]{:S(2)}) collective-permute-start(bf16[35,4096]{1,0:T(8,128)(2,1)S(1)} %constant_dynamic-update-slice_fusion), channel_id=1, source_target_pairs={{1,0},{2,1},{3,2},{4,3},{5,4},{6,5},{7,6},{8,7},{9,8},{10,9},{11,1... | collective-permute-start | bytes 860168 | tf_op jit(solution)/shard_map/ppermute | solution.py:18
  9.7 191.5 %collective-permute-start = (bf16[35,4096]{1,0:T(8,128)(2,1)S(1)}, bf16[35,4096]{1,0:T(8,128)(2,1)S(1)}, u32[]{:S(2)}, u32[]{:S(2)}) collective-permute-start(bf16[35,4096]{1,0:T(8,128)(2,1)S(1)} %constant_dynamic-update-slice_fusion), channel_id=1, source_target_pairs={{0,1},{1,2},{2,3},{3,4},{4,5},{5,6},{6,7},{7,8},{8,9},{9,10},{10,1... | collective-permute-start | bytes 860168 | tf_op jit(solution)/shard_map/ppermute | solution.py:17
  16.1 185.4 %copy-start.2 = (s32[16]{0:T(128)S(1)}, s32[16]{0:T(128)}, u32[]{:S(2)}) copy-start(s32[16]{0:T(128)} %param.17) | copy-start | bytes 196
  98.8 26.4 %all-to-all-start = ((bf16[32,2,1024]{2,1,0:T(2,128)(2,1)}), bf16[32,2,1024]{2,1,0:T(2,128)(2,1)S(1)}, u32[]{:S(2)}, u32[]{:S(2)}) async-start(bf16[32,2,1024]{2,1,0:T(2,128)(2,1)} %reshape.569), calls=%async_computation | async-start | bytes 262144 | tf_op jit(solution)/shard_map/all_to_all | solution.py:112
  353.0 3.8 %copy-start.1 = (bf16[16,64,64]{2,1,0:T(8,128)(2,1)S(1)}, bf16[16,64,64]{2,1,0:T(8,128)(2,1)}, u32[]{:S(2)}) copy-start(bf16[16,64,64]{2,1,0:T(8,128)(2,1)} %param.22) | copy-start | bytes 393220
Sparse Core Ops, SparseCore 0:
  16.3 92.3 all-gather.1
